TPU v7x, 32 devices: a whole 2x2x4 slice. The times are simulated.
32 devices in a mesh: dp: 16 (over z, y, core), tensor: 2 (over x).
Axes of the slice: x: 2, y: 2, z: 4, core: 2. Of those that a mesh axis runs over, the one named last changes fastest.
Arguments:
- prefix_kv: bfloat16 [32768, 2048], P('dp', 'tensor'), may hold values from -24 to 24
- page_key_values: bfloat16 [512, 256, 2048], P('dp', None, 'tensor'), may hold values from -6 to 6
- context_len: int32 [512], P('dp'), may hold values from 1 to 256
- prefill_owner: int32 [1], replicated, may hold values from 0 to 15
- assign: int32 [512, 1], P('dp'), may hold values from 0 to 15, as said below
- x_new: bfloat16 [512, 4, 8192], P('dp', None, 'tensor'), may hold values from -6 to 6
- norm_gain: float32 [8192], replicated, may hold values from 0.1 to 1.9
- key_weight: bfloat16 [8192, 1024], P(None, 'tensor'), may hold values from -0.25 to 0.25
- value_weight: bfloat16 [8192, 1024], P(None, 'tensor'), may hold values from -0.0625 to 0.0625
- decoded_queries: bfloat16 [512, 4, 8192], P('dp', None, 'tensor'), may hold values from -30 to 30
Outputs:
- decoded: bfloat16 [512, 4, 8192], P('dp', None, 'tensor')
Inputs may be any that keep to these rules, and one draw needn't show every extreme that they name: `assign`: within the 32 requests of one device no group is named more than 2 times; one group, the same for every device, is named exactly 2 times by the requests of every device.
All inputs are finite; a program needn't handle non-finite values.
Results may differ from a plain program's by a relative error of at most 0.0088.
Values may be sent and summed in bfloat16 or wider, within the bound.
A program may use at most 192 MiB of HBM per device.

v0:
```python
import math

import jax
import jax.numpy as jnp
from jax import lax
from jax.sharding import PartitionSpec as P

HEAD_SIZE = 128
CAP = 2


epsilon = 1e-05


def broadcast(block, axis, holder):
    block = jnp.where(lax.axis_index(axis) == holder, block, jnp.zeros_like(block))
    return lax.psum(block, axis)


def attend(queries, page_rows, recent_key_values, request_lengths, prefix):
    members = queries.shape[0]
    step_count = queries.shape[1]
    key_heads = prefix.shape[1] // (2 * HEAD_SIZE)
    group_size = queries.shape[2] // (key_heads * HEAD_SIZE)
    page_span = page_rows.shape[1]
    grouped = queries.reshape(members, step_count, key_heads, group_size, HEAD_SIZE)
    shared = prefix.reshape(prefix.shape[0], key_heads, 2, HEAD_SIZE)
    paged = page_rows.reshape(members, page_span, key_heads, 2, HEAD_SIZE)
    recent = recent_key_values.reshape(members, step_count, key_heads, 2, HEAD_SIZE)
    scaling = 1.0 / math.sqrt(HEAD_SIZE)
    shared_scores = (
        jnp.einsum("ntjgd,ljd->ntjgl", grouped, shared[:, :, 0], preferred_element_type=jnp.float32)
        * scaling
    )
    paged_scores = (
        jnp.einsum(
            "ntjgd,npjd->ntjgp", grouped, paged[:, :, :, 0], preferred_element_type=jnp.float32
        )
        * scaling
    )
    recent_scores = (
        jnp.einsum(
            "ntjgd,nsjd->ntjgs", grouped, recent[:, :, :, 0], preferred_element_type=jnp.float32
        )
        * scaling
    )
    position = jnp.arange(page_span).astype(jnp.float32)
    visible = position[None, :] < request_lengths[:, None]
    paged_scores = jnp.where(visible[:, None, None, None, :], paged_scores, -jnp.inf)
    causal = jnp.arange(step_count)[None, :] <= jnp.arange(step_count)[:, None]
    recent_scores = jnp.where(causal[None, :, None, None, :], recent_scores, -jnp.inf)
    highest = jnp.maximum(
        jnp.maximum(
            jnp.max(shared_scores, axis=-1, keepdims=True),
            jnp.max(paged_scores, axis=-1, keepdims=True),
        ),
        jnp.max(recent_scores, axis=-1, keepdims=True),
    )
    shared_exp = jnp.exp(shared_scores - highest)
    paged_exp = jnp.exp(paged_scores - highest)
    recent_exp = jnp.exp(recent_scores - highest)
    denominator = (
        jnp.sum(shared_exp, axis=-1, keepdims=True)
        + jnp.sum(paged_exp, axis=-1, keepdims=True)
        + jnp.sum(recent_exp, axis=-1, keepdims=True)
    )
    shared_weights = (shared_exp / denominator).astype(jnp.bfloat16)
    paged_weights = (paged_exp / denominator).astype(jnp.bfloat16)
    recent_weights = (recent_exp / denominator).astype(jnp.bfloat16)
    result = jnp.einsum(
        "ntjgl,ljd->ntjgd", shared_weights, shared[:, :, 1], preferred_element_type=jnp.float32
    )
    result = result + jnp.einsum(
        "ntjgp,npjd->ntjgd", paged_weights, paged[:, :, :, 1], preferred_element_type=jnp.float32
    )
    result = result + jnp.einsum(
        "ntjgs,nsjd->ntjgd", recent_weights, recent[:, :, :, 1], preferred_element_type=jnp.float32
    )
    return result.reshape(members, step_count, key_heads * group_size * HEAD_SIZE).astype(
        jnp.bfloat16
    )


def per_device(
    prefix_kv,
    page_key_values,
    context_len,
    prefill_owner,
    assign,
    x_new,
    norm_gain,
    key_weight,
    value_weight,
    decoded_queries,
):
    row_count = decoded_queries.shape[0]
    step_count = decoded_queries.shape[1]
    features = lax.all_gather(x_new, "tensor", axis=2, tiled=True).astype(jnp.float32)
    normed = (
        features
        * lax.rsqrt(jnp.mean(features * features, axis=2, keepdims=True) + epsilon)
        * norm_gain
    ).astype(jnp.bfloat16)
    flattened = normed.reshape(row_count * step_count, features.shape[2])
    fresh_keys = jnp.dot(flattened, key_weight, preferred_element_type=jnp.float32).astype(
        jnp.bfloat16
    )
    fresh_values = jnp.dot(flattened, value_weight, preferred_element_type=jnp.float32).astype(
        jnp.bfloat16
    )
    key_heads = key_weight.shape[1] // HEAD_SIZE
    recent_key_values = jnp.stack(
        [
            fresh_keys.reshape(row_count, step_count, key_heads, HEAD_SIZE),
            fresh_values.reshape(row_count, step_count, key_heads, HEAD_SIZE),
        ],
        axis=3,
    ).reshape(row_count, step_count, 2 * key_heads * HEAD_SIZE)
    prefix = broadcast(prefix_kv, "dp", prefill_owner[0])
    group_count = lax.axis_size("dp")
    assigned = assign[:, 0]
    indices = jnp.arange(row_count)
    matching = (assigned[:, None] == assigned[None, :]) & (indices[None, :] < indices[:, None])
    ranking = jnp.sum(matching.astype(jnp.int32), axis=1)
    destination = assigned * CAP + ranking
    selector = (jnp.arange(group_count * CAP)[:, None] == destination[None, :]).astype(jnp.bfloat16)

    def to_slots(payload):
        arranged = jnp.dot(
            selector, payload.reshape(row_count, -1), preferred_element_type=jnp.bfloat16
        )
        return arranged.reshape((group_count, CAP) + payload.shape[1:])

    request_lengths = context_len.astype(jnp.bfloat16)[:, None]
    page_rows = lax.all_to_all(
        to_slots(page_key_values), "dp", split_axis=0, concat_axis=0, tiled=True
    )
    queries = lax.all_to_all(
        to_slots(decoded_queries), "dp", split_axis=0, concat_axis=0, tiled=True
    )
    recent_in = lax.all_to_all(
        to_slots(recent_key_values), "dp", split_axis=0, concat_axis=0, tiled=True
    )
    lengths_in = lax.all_to_all(
        to_slots(request_lengths), "dp", split_axis=0, concat_axis=0, tiled=True
    )
    members = page_rows.shape[0] * page_rows.shape[1]
    sizes_flat = lengths_in.reshape(members)
    result = attend(
        queries.reshape((members,) + queries.shape[2:]),
        page_rows.reshape((members,) + page_rows.shape[2:]),
        recent_in.reshape((members,) + recent_in.shape[2:]),
        sizes_flat.astype(jnp.float32),
        prefix,
    )
    result = result * (sizes_flat > 0).astype(jnp.bfloat16)[:, None, None]
    decoded = result.reshape(page_rows.shape[0], page_rows.shape[1], step_count, result.shape[2])
    return decoded.reshape(group_count * CAP, step_count, decoded.shape[3])


def solution(mesh):
    in_specs = (
        P("dp", "tensor"),
        P("dp", None, "tensor"),
        P("dp"),
        P(),
        P("dp", None),
        P("dp", None, "tensor"),
        P(),
        P(None, "tensor"),
        P(None, "tensor"),
        P("dp", None, "tensor"),
    )
    out_specs = P("dp", None, "tensor")
    return jax.shard_map(
        per_device, mesh=mesh, in_specs=in_specs, out_specs=out_specs, check_vma=False
    )
```

profile of v0, /device:TPU:0, one launch (start us, length us, event | category | flops | bytes accessed | tf_op | source)
XLA Modules:
  0.0 669.4 jit_solution(16039544672136306466)
XLA Ops:
  7.4 0.7 all-gather.2.cloned.1.call-update
  8.1 0.9 convert_reduce_fusion
  9.0 0.7 multiply_add_fusion.1
  9.7 0.8 fusion.32
  10.5 0.1 copy.202
  10.6 0.7 copy.172
  11.3 7.4 %all-to-all-start.1 = ((bf16[16,2,1]{1,2,0:T(2,128)(2,1)}), bf16[16,2,1]{1,2,0:T(2,128)(2,1)S(1)}, u32[]{:S(2)}, u32[]{:S(2)}) async-start(bf16[16,2,1]{1,2,0:T(2,128)(2,1)} %copy.172), calls=%async_computation.1 | async-start | bytes 16384 | tf_op jit(solution)/shard_map/all_to_all | solution.py:144
  18.7 0.0 copy-start.2
  18.7 2.8 fusion.21
  21.5 1.8 copy.170
  23.3 22.3 %all-gather.2.cloned.1.call-done = bf16[32,4,8192]{2,1,0:T(4,128)(2,1)} async-done(((bf16[32,4,4096]{2,1,0:T(4,128)(2,1)}), bf16[32,4,8192]{2,1,0:T(4,128)(2,1)}) %all-gather.2.cloned.1.call-update) | async-done | bytes 2097168 | tf_op jit(solution)/shard_map/all_gather | solution.py:98
  45.6 2.9 fusion.7
  48.6 0.0 all-to-all-done.1
  48.6 5.6 all-to-all-start
  54.2 2.6 fusion.9
  56.8 2.5 reshape.179
  59.4 4.6 convolution_convert_fusion.1
  64.0 0.1 stack_reshape.8
  64.1 4.6 convolution_convert_fusion
  68.8 0.1 stack_reshape.9
  68.8 0.6 pad_maximum_fusion
  69.4 0.2 reshape_reshape.14
  69.6 0.3 fusion.30
  69.9 0.9 copy.184
  70.8 6.4 all-to-all-done
  77.2 7.0 %all-to-all-start.3 = ((bf16[16,2,4,1024]{3,2,1,0:T(4,128)(2,1)}), bf16[16,2,4,1024]{3,2,1,0:T(4,128)(2,1)S(1)}, u32[]{:S(2)}, u32[]{:S(2)}) async-start(bf16[16,2,4,1024]{3,2,1,0:T(4,128)(2,1)} %copy.184), calls=%async_computation.3 | async-start | bytes 524288 | tf_op jit(solution)/shard_map/all_to_all | solution.py:141
  84.2 23.1 %fusion.2 = bf16[16,2,256,1024]{3,0,2,1:T(8,128)(2,1)} fusion(s32[32]{0:T(128)S(1)} %multiply_add_fusion.1, s32[16,2]{0,1:T(2,128)S(1)} %multiply_add_fusion, bf16[4,8,256,1024]{3,2,1,0:T(8,128)(2,1)} %bitcast.146), kind=kOutput, calls=%fused_computation.6 | convolution fusion | flops 536871936 | bytes 33554688 | tf_op jit(solution)/shard_map/dot_general | solution.py:129
  107.3 18.7 %copy.174 = bf16[16,2,256,1024]{3,2,1,0:T(8,128)(2,1)} copy(bf16[16,2,256,1024]{3,0,2,1:T(8,128)(2,1)} %fusion.2) | data formatting | bytes 33554432 | tf_op jit(solution)/shard_map/dot_general | solution.py:129
  126.0 0.0 all-to-all-done.3
  126.0 6.2 all-to-all-start.2
  132.2 0.3 all-reduce.2.cloned.1.call-start
  133.1 6.5 copy.167
  139.6 2.2 broadcast_select_fusion
  141.9 6.2 copy.168
  148.1 0.0 all-reduce.2.cloned.1.call-update
  148.2 0.1 reshape.181
  148.3 0.1 reshape.180
  148.4 0.1 broadcast_compare_fusion
  148.5 1.1 reshape_reshape.12
  149.6 418.6 %all-reduce.2.cloned.1.call-done = bf16[2048,4,2,128]{3,0,1,2:T(8,128)(2,1)} async-done(((bf16[2048,4,2,128]{3,0,1,2:T(8,128)(2,1)}), bf16[2048,4,2,128]{3,0,1,2:T(8,128)(2,1)}) %all-reduce.2.cloned.1.call-update) | async-done | bytes 4194320 | tf_op jit(solution)/shard_map/psum | solution.py:17
  568.2 14.8 %bitcast_reduce_fusion = (f32[32,4,4,8]{0,3,1,2:T(8,128)S(1)}, f32[4,2048,32,4,8]{1,2,4,3,0:T(8,128)}) fusion(bf16[32,4,4,8,128]{4,3,2,1,0:T(8,128)(2,1)S(1)} %reshape_reshape.12, bf16[2048,4,2,128]{3,0,1,2:T(8,128)(2,1)} %all-reduce.2.cloned.1.call-done), kind=kOutput, calls=%fused_computation.1 | convolution fusion | flops 2164256768 | bytes 36716544 | tf_op jit(solution)/shard_map/ntjgd,ljd->ntjgl/dot_general | solution.py:32
  583.0 0.1 reshape_reshape.15
  583.1 0.4 fusion.49
  583.5 4.7 fusion.50
  588.2 0.2 copy.187
  588.3 0.0 all-to-all-done.2
  588.3 21.5 %copy.175 = bf16[16,2,256,1024]{2,3,1,0:T(8,128)(2,1)} copy(bf16[16,2,256,1024]{3,2,1,0:T(8,128)(2,1)} %all-to-all-done.2) | data formatting | bytes 33554432 | tf_op jit(solution)/shard_map/all_to_all | solution.py:135
  609.9 6.9 %bitcast_reduce_fusion.1 = (f32[32,4,4,8]{3,1,2,0:T(4,128)S(1)}, f32[32,4,256,4,8]{2,4,3,1,0:T(8,128)}) fusion(pred[32,256]{1,0:T(8,128)(4,1)S(1)} %broadcast_compare_fusion, bf16[32,4,4,8,128]{4,3,2,1,0:T(8,128)(2,1)S(1)} %reshape_reshape.12, bf16[32,256,4,2,128]{1,4,3,2,0:T(8,128)(2,1)} %bitcast.147), kind=kOutput, calls=%fused_computation.19 | convolution fusion | flops 271577088 | bytes 13656064 | tf_op jit(solution)/shard_map/ntjgd,npjd->ntjgp/dot_general | solution.py:36
  616.8 0.2 copy.178
  617.0 0.2 copy.188
  617.2 14.3 %fusion.1 = f32[32,4,4,8]{0,3,1,2:T(8,128)S(1)} fusion(f32[4,2048,32,4,8]{1,2,4,3,0:T(8,128)} %get-tuple-element.10, f32[32,4,4,8]{0,3,1,2:T(8,128)S(1)} %maximum_maximum_fusion), kind=kLoop, calls=%fused_computation.4 | loop fusion | flops 25161728 | bytes 33587200 | tf_op jit(solution)/shard_map/reduce_sum | solution.py:63
  631.5 1.0 fusion.26
  632.5 0.2 copy.191
  632.6 3.2 fusion.11
  635.8 0.2 copy.189
  635.9 0.2 copy.193
  636.1 6.2 fusion.5
  642.3 0.8 fusion.27
  643.1 1.4 copy-done.1
  644.5 14.2 %fusion.13 = bf16[32,4,4,8,128]{4,0,3,1,2:T(8,128)(2,1)S(1)} fusion(f32[32,4,128,4,8]{2,4,3,1,0:T(8,128)S(1)} %fusion.27, f32[32,4,128,4,8]{2,4,3,1,0:T(8,128)S(1)} %fusion.5, f32[4,2048,32,4,8]{1,2,4,3,0:T(8,128)} %get-tuple-element.10, f32[32,4,4,8]{0,3,1,2:T(8,128)S(1)} %add_add_fusion, f32[32,4,4,8]{0,3,1,2:T(8,128)S(1)} %maximum_maximum_fusion, ...), kind=kOutput, calls=%fused_computation.29 | convolution fusion | flops 2182610944 | bytes 41025536 | tf_op jit(solution)/shard_map/ntjgl,ljd->ntjgd/dot_general | solution.py:70
  658.7 0.4 copy.198
  659.1 0.5 convert_element_type.74
  659.6 0.1 broadcast_multiply_fusion
  659.8 1.8 copy.199
  (13 shorter events, 0.1 us)
Async XLA Ops:
  7.4 38.3 %all-gather.2.cloned.1.call-start = ((), (), s32[]{:S(2)}) async-start(), calls=%async_computation.5 | async-start | bytes 3145728 | tf_op jit(solution)/shard_map/all_gather | solution.py:98
  11.3 37.3 %all-to-all-start.1 = ((bf16[16,2,1]{1,2,0:T(2,128)(2,1)}), bf16[16,2,1]{1,2,0:T(2,128)(2,1)S(1)}, u32[]{:S(2)}, u32[]{:S(2)}) async-start(bf16[16,2,1]{1,2,0:T(2,128)(2,1)} %copy.172), calls=%async_computation.1 | async-start | bytes 16384 | tf_op jit(solution)/shard_map/all_to_all | solution.py:144
  18.7 35.5 %copy-start.2 = (f32[8192]{0:T(1024)S(1)}, f32[8192]{0:T(1024)}, u32[]{:S(2)}) copy-start(f32[8192]{0:T(1024)} %param.16) | copy-start | bytes 98308
  45.6 8.6 %copy-start = (bf16[32,4,8192]{2,1,0:T(4,128)(2,1)S(1)}, bf16[32,4,8192]{2,1,0:T(4,128)(2,1)}, u32[]{:S(2)}) copy-start(bf16[32,4,8192]{2,1,0:T(4,128)(2,1)} %all-gather.2.cloned.1.call-done) | copy-start | bytes 6291460
  48.6 28.6 %all-to-all-start = ((bf16[16,2,4,4096]{3,2,1,0:T(4,128)(2,1)}), bf16[16,2,4,4096]{3,2,1,0:T(4,128)(2,1)S(1)}, u32[]{:S(2)}, u32[]{:S(2)}) async-start(bf16[16,2,4,4096]{3,2,1,0:T(4,128)(2,1)} %copy.170), calls=%async_computation | async-start | bytes 2097152 | tf_op jit(solution)/shard_map/all_to_all | solution.py:138
  77.2 48.8 %all-to-all-start.3 = ((bf16[16,2,4,1024]{3,2,1,0:T(4,128)(2,1)}), bf16[16,2,4,1024]{3,2,1,0:T(4,128)(2,1)S(1)}, u32[]{:S(2)}, u32[]{:S(2)}) async-start(bf16[16,2,4,1024]{3,2,1,0:T(4,128)(2,1)} %copy.184), calls=%async_computation.3 | async-start | bytes 524288 | tf_op jit(solution)/shard_map/all_to_all | solution.py:141
  126.0 462.3 %all-to-all-start.2 = ((bf16[16,2,256,1024]{3,2,1,0:T(8,128)(2,1)}), bf16[16,2,256,1024]{3,2,1,0:T(8,128)(2,1)}, u32[]{:S(2)}, u32[]{:S(2)}) async-start(bf16[16,2,256,1024]{3,2,1,0:T(8,128)(2,1)} %copy.174), calls=%async_computation.2 | async-start | bytes 33554432 | tf_op jit(solution)/shard_map/all_to_all | solution.py:135
  132.2 436.0 %all-reduce.2.cloned.1.call-start = ((), (), s32[]{:S(2)}) async-start(), calls=%async_computation.4 | async-start | bytes 8388608 | tf_op jit(solution)/shard_map/psum | solution.py:17
  642.3 2.2 copy-start.1
Sparse Core Ops, SparseCore 0:
  9.7 35.8 all-gather.1
Sparse Core Ops, SparseCore 1:
  148.2 419.9 all-reduce.1
where the time goes:
time: 678 us; the launch traced here: 669 us
  waiting for transfers between devices  448 us (66%)
  matrix products  83.9 us (12%)
  local copies, waits for them, and re-layouts  66.2 us (10%)
  other arithmetic  28.7 us (4%)
  starting transfers between devices  26.5 us (4%)
  between operations  16.2 us (2%)
    psum x1, waiting for transfers between devices, broadcast(): return lax.psum(block, axis)  419 us
    dot_general x4, matrix products, to_slots(): jnp.dot(selector, payload.reshape(row_count, -1), preferred_element_type=...  27.1 us
    all_gather x1, waiting for transfers between devices, per_device(): lax.all_gather(x_new, 'tensor', axis=2, tiled=True).astype(jnp.float32)  22.3 us
    dot_general x5, local copies, waits for them, and re-layouts, to_slots(): jnp.dot(selector, payload.reshape(row_count, -1), preferred_element_type=...  22.2 us
    all_to_all x1, local copies, waits for them, and re-layouts, per_device(): lax.all_to_all(to_slots(page_key_values), 'dp', split_axis=0, concat_axis...  21.5 us
    dot_general x1, matrix products, attend(): jnp.einsum('ntjgd,ljd->ntjgl', grouped, shared[:, :, 0], preferred_elemen...  14.8 us
    reduce_sum x1, other arithmetic, attend(): jnp.sum(shared_exp, axis=-1, keepdims=True)  14.3 us
    dot_general x1, matrix products, attend(): jnp.einsum('ntjgl,ljd->ntjgd', shared_weights, shared[:, :, 1], preferred...  14.2 us
  transfers between devices with their start and end apart: 6, of which 3 were waited for; matrix products, arithmetic and copies ran while one was open for 16% of the time, Pallas kernels for 0%

commit v1 on v0

v1 whole, which is shorter than its diff:
```python
import functools
import math

import jax
import jax.numpy as jnp
from jax import lax
from jax.experimental import pallas as pl
from jax.experimental.pallas import tpu as pltpu
from jax.sharding import PartitionSpec as P

HEAD_SIZE = 128
CAP = 2
epsilon = 1e-05
SCALE2 = math.log2(math.e) / math.sqrt(HEAD_SIZE)
VMEM_LIMIT = 56 * 1024 * 1024
NT = (((1,), (1,)), ((), ()))


def broadcast(block, axis, holder):
    block = jnp.where(lax.axis_index(axis) == holder, block, jnp.zeros_like(block))
    return lax.psum(block, axis)


def page_kernel(key_heads, group, steps, span, len_ref, q_ref, page_ref, acc_ref, top_ref, sum_ref):
    i = pl.program_id(0)
    tile = q_ref.shape[0]
    per_pair = 8 // steps
    queries = q_ref[...].astype(jnp.float32)
    rows = group * 8
    keys = per_pair * span
    row = lax.broadcasted_iota(jnp.int32, (rows, keys), 0)
    col = lax.broadcasted_iota(jnp.int32, (rows, keys), 1)
    owner = (row % 8) // steps
    for p in range(tile // 8):
        limit = jnp.zeros((rows, keys), jnp.int32)
        for k in range(per_pair):
            used = len_ref[i * (tile // steps) + p * per_pair + k]
            limit = jnp.where(owner == k, used, limit)
        place = col - owner * span
        visible = (place >= 0) & (place < limit)
        base = p * per_pair
        for j in range(key_heads):
            q = jnp.concatenate(
                [
                    queries[p * 8 : p * 8 + 8, (j * group + g) * HEAD_SIZE : (j * group + g + 1) * HEAD_SIZE]
                    for g in range(group)
                ],
                axis=0,
            ).astype(jnp.bfloat16)
            c = 2 * j * HEAD_SIZE
            k = page_ref[base : base + per_pair, :, c : c + HEAD_SIZE].reshape(keys, HEAD_SIZE)
            v = page_ref[base : base + per_pair, :, c + HEAD_SIZE : c + 2 * HEAD_SIZE].reshape(keys, HEAD_SIZE)
            s = lax.dot_general(q, k, NT, preferred_element_type=jnp.float32)
            s = jnp.where(visible, s, -jnp.inf)
            top = jnp.max(s, axis=1, keepdims=True)
            e = jnp.exp2((s - top) * SCALE2)
            total = jnp.sum(e, axis=1, keepdims=True)
            acc = jnp.dot(e.astype(jnp.bfloat16), v, preferred_element_type=jnp.float32)
            top = jnp.broadcast_to(top, acc.shape)
            total = jnp.broadcast_to(total, acc.shape)
            for g in range(group):
                acc_ref[j, g, p * 8 : p * 8 + 8, :] = acc[g * 8 : g * 8 + 8]
                top_ref[j, g, p * 8 : p * 8 + 8, :] = top[g * 8 : g * 8 + 8]
                sum_ref[j, g, p * 8 : p * 8 + 8, :] = total[g * 8 : g * 8 + 8]


def page_part(queries, pages, lengths, steps):
    tokens, width = queries.shape
    members, span, kv_width = pages.shape
    key_heads = kv_width // (2 * HEAD_SIZE)
    group = width // (key_heads * HEAD_SIZE)
    tile = 16
    grid = tokens // tile
    shape = jax.ShapeDtypeStruct((key_heads, group, tokens, HEAD_SIZE), jnp.float32)
    spec = pl.BlockSpec((key_heads, group, tile, HEAD_SIZE), lambda i: (0, 0, i, 0))
    return pl.pallas_call(
        functools.partial(page_kernel, key_heads, group, steps, span),
        grid=(grid,),
        in_specs=[
            pl.BlockSpec(memory_space=pltpu.SMEM),
            pl.BlockSpec((tile, width), lambda i: (i, 0)),
            pl.BlockSpec((tile // steps, span, kv_width), lambda i: (i, 0, 0)),
        ],
        out_specs=[spec] * 3,
        out_shape=[shape] * 3,
        compiler_params=pltpu.CompilerParams(vmem_limit_bytes=VMEM_LIMIT),
        cost_estimate=pl.CostEstimate(
            flops=16 * tokens * span * width, bytes_accessed=2 * pages.size, transcendentals=0
        ),
    )(lengths, queries, pages)


def prefix_kernel(group, steps, q_ref, kv_ref, nk_ref, nv_ref, acc_ref, top_ref, sum_ref, out_ref):
    tokens = q_ref.shape[0]
    keys = kv_ref[:, :HEAD_SIZE]
    values = kv_ref[:, HEAD_SIZE:]
    wide = 2
    row = lax.broadcasted_iota(jnp.int32, (wide * tokens, tokens), 0) % tokens
    col = lax.broadcasted_iota(jnp.int32, (wide * tokens, tokens), 1)
    visible = (row // steps == col // steps) & (col <= row)
    for g in range(0, group, wide):
        q = jnp.concatenate(
            [q_ref[:, (g + w) * HEAD_SIZE : (g + w + 1) * HEAD_SIZE] for w in range(wide)], axis=0
        )
        paged = jnp.concatenate([acc_ref[0, g + w] for w in range(wide)], axis=0)
        paged_top = jnp.concatenate([top_ref[0, g + w][:, :1] for w in range(wide)], axis=0)
        paged_sum = jnp.concatenate([sum_ref[0, g + w][:, :1] for w in range(wide)], axis=0)
        s = lax.dot_general(q, keys, NT, preferred_element_type=jnp.float32)
        r = lax.dot_general(q, nk_ref[...], NT, preferred_element_type=jnp.float32)
        r = jnp.where(visible, r, -jnp.inf)
        top = jnp.maximum(jnp.max(s, axis=1, keepdims=True), jnp.max(r, axis=1, keepdims=True))
        top = jnp.maximum(top, paged_top)
        e = jnp.exp2((s - top) * SCALE2)
        f = jnp.exp2((r - top) * SCALE2)
        keep = jnp.exp2((paged_top - top) * SCALE2)
        total = (
            jnp.sum(e, axis=1, keepdims=True) + jnp.sum(f, axis=1, keepdims=True) + keep * paged_sum
        )
        acc = jnp.dot(e.astype(jnp.bfloat16), values, preferred_element_type=jnp.float32)
        acc += jnp.dot(f.astype(jnp.bfloat16), nv_ref[...], preferred_element_type=jnp.float32)
        acc = (acc + keep * paged) / total
        for w in range(wide):
            out_ref[:, (g + w) * HEAD_SIZE : (g + w + 1) * HEAD_SIZE] = acc[
                w * tokens : (w + 1) * tokens
            ].astype(jnp.bfloat16)


def prefix_part(queries, prefix, new_keys, new_values, paged, steps):
    tokens, width = queries.shape
    length, kv_width = prefix.shape
    key_heads = kv_width // (2 * HEAD_SIZE)
    group = width // (key_heads * HEAD_SIZE)
    part = pl.BlockSpec((1, group, tokens, HEAD_SIZE), lambda j: (j, 0, 0, 0))
    return pl.pallas_call(
        functools.partial(prefix_kernel, group, steps),
        grid=(key_heads,),
        in_specs=[
            pl.BlockSpec((tokens, group * HEAD_SIZE), lambda j: (0, j)),
            pl.BlockSpec((length, 2 * HEAD_SIZE), lambda j: (0, j)),
            pl.BlockSpec((tokens, HEAD_SIZE), lambda j: (0, j)),
            pl.BlockSpec((tokens, HEAD_SIZE), lambda j: (0, j)),
            part,
            part,
            part,
        ],
        out_specs=pl.BlockSpec((tokens, group * HEAD_SIZE), lambda j: (0, j)),
        out_shape=jax.ShapeDtypeStruct((tokens, width), jnp.bfloat16),
        compiler_params=pltpu.CompilerParams(vmem_limit_bytes=VMEM_LIMIT),
        cost_estimate=pl.CostEstimate(
            flops=4 * tokens * length * width, bytes_accessed=2 * prefix.size, transcendentals=0
        ),
    )(queries, prefix, new_keys, new_values, *paged)


def per_device(
    prefix_kv,
    page_key_values,
    context_len,
    prefill_owner,
    assign,
    x_new,
    norm_gain,
    key_weight,
    value_weight,
    decoded_queries,
):
    row_count, step_count, width = decoded_queries.shape
    tokens = row_count * step_count
    prefix = broadcast(prefix_kv, "dp", prefill_owner[0])
    features = lax.all_gather(x_new, "tensor", axis=2, tiled=True).astype(jnp.float32)
    normed = (
        features
        * lax.rsqrt(jnp.mean(features * features, axis=2, keepdims=True) + epsilon)
        * norm_gain
    ).astype(jnp.bfloat16)
    flattened = normed.reshape(tokens, features.shape[2])
    new_keys = jnp.dot(flattened, key_weight, preferred_element_type=jnp.float32).astype(jnp.bfloat16)
    new_values = jnp.dot(flattened, value_weight, preferred_element_type=jnp.float32).astype(
        jnp.bfloat16
    )
    queries = decoded_queries.reshape(tokens, width)
    paged = page_part(queries, page_key_values, context_len, step_count)
    attended = prefix_part(queries, prefix, new_keys, new_values, paged, step_count)

    group_count = lax.axis_size("dp")
    assigned = assign[:, 0]
    indices = jnp.arange(row_count)
    matching = (assigned[:, None] == assigned[None, :]) & (indices[None, :] < indices[:, None])
    ranking = jnp.sum(matching.astype(jnp.int32), axis=1)
    destination = assigned * CAP + ranking
    selector = (jnp.arange(group_count * CAP)[:, None] == destination[None, :]).astype(jnp.bfloat16)
    arranged = jnp.dot(
        selector, attended.reshape(row_count, -1), preferred_element_type=jnp.bfloat16
    ).reshape(group_count, CAP, step_count, width)
    decoded = lax.all_to_all(arranged, "dp", split_axis=0, concat_axis=0, tiled=True)
    return decoded.reshape(group_count * CAP, step_count, width)


def solution(mesh):
    in_specs = (
        P("dp", "tensor"),
        P("dp", None, "tensor"),
        P("dp"),
        P(),
        P("dp", None),
        P("dp", None, "tensor"),
        P(),
        P(None, "tensor"),
        P(None, "tensor"),
        P("dp", None, "tensor"),
    )
    out_specs = P("dp", None, "tensor")
    return jax.shard_map(
        per_device, mesh=mesh, in_specs=in_specs, out_specs=out_specs, check_vma=False
    )
```

time: 678 us -> 186 us (0.27); the launches traced: 669 us -> 185 us
  waiting for transfers between devices: 448 us -> 72.4 us
  matrix products: 83.9 us -> 11.2 us
  local copies, waits for them, and re-layouts: 66.2 us -> 8.5 us
  Pallas kernels: 0 us -> 39.5 us
  blocking collectives: 0 us -> 28.3 us
  starting transfers between devices: 26.5 us -> 0.05 us
  other arithmetic: 28.7 us -> 9.69 us
    psum x1, waiting for transfers between devices: 419 us -> 59.9 us  [broadcast(): return lax.psum(block, axis)]
    dot_general x10 -> x1, matrix products: 74.6 us -> 0.49 us  [per_device(): jnp.dot(selector, attended.reshape(row_count, -1), preferred_element_type...]
    pallas_call x0 -> x2, Pallas kernels: none -> 39.5 us  [the longest x1 20.4 us: page_part(): pl.pallas_call(functools.partial(page_kernel, key_heads, group, steps, sp...]
    all_to_all x0 -> x1, blocking collectives: none -> 28.3 us  [per_device(): lax.all_to_all(arranged, 'dp', split_axis=0, concat_axis=0, tiled=True)]
    all_to_all x4 -> x0, starting transfers between devices: 26.2 us -> none  [the longest x1 7.39 us: per_device(): lax.all_to_all(to_slots(request_lengths), 'dp', split_axis=0, concat_axis...]
    all_to_all x1 -> x0, local copies, waits for them, and re-layouts: 21.5 us -> none  [per_device(): lax.all_to_all(to_slots(page_key_values), 'dp', split_axis=0, concat_axis...]
    dot_general x5 -> x1, local copies, waits for them, and re-layouts: 22.2 us -> 0.81 us  [per_device(): jnp.dot(selector, attended.reshape(row_count, -1), preferred_element_type...]
    reduce_sum x3 -> x0, other arithmetic: 18.4 us -> none  [the longest x1 14.3 us: attend(): jnp.sum(shared_exp, axis=-1, keepdims=True)]
  transfers between devices with their start and end apart: 6 -> 2, of which waited for: 3 -> 2; matrix products, arithmetic and copies ran while one was open for 16% -> 13% of each run, Pallas kernels for 0% -> 11%
where the time goes in v1:
time: 186 us; the launch traced here: 185 us
  waiting for transfers between devices  72.4 us (39%)
  Pallas kernels  39.5 us (21%)
  blocking collectives  28.3 us (15%)
  between operations  15.5 us (8%)
  matrix products  11.2 us (6%)
  other arithmetic  9.69 us (5%)
  local copies, waits for them, and re-layouts  8.5 us (5%)
    psum x1, waiting for transfers between devices, broadcast(): return lax.psum(block, axis)  59.9 us
    all_to_all x1, blocking collectives, per_device(): lax.all_to_all(arranged, 'dp', split_axis=0, concat_axis=0, tiled=True)  28.3 us
    pallas_call x1, Pallas kernels, page_part(): pl.pallas_call(functools.partial(page_kernel, key_heads, group, steps, sp...  20.4 us
    pallas_call x1, Pallas kernels, prefix_part(): pl.pallas_call(functools.partial(prefix_kernel, group, steps), grid=(key_...  19.1 us
    all_gather x1, waiting for transfers between devices, per_device(): lax.all_gather(x_new, 'tensor', axis=2, tiled=True).astype(jnp.float32)  11.8 us
    dot_general x1, matrix products, per_device(): jnp.dot(flattened, key_weight, preferred_element_type=jnp.float32)  5.43 us
    dot_general x1, matrix products, per_device(): jnp.dot(flattened, value_weight, preferred_element_type=jnp.float32)  5.33 us
    convert_element_type x1, other arithmetic, per_device(): normed = (features * lax.rsqrt(jnp.mean(features * features, axis=2, keep...  4.42 us
  transfers between devices with their start and end apart: 2, of which 2 were waited for; matrix products, arithmetic and copies ran while one was open for 13% of the time, Pallas kernels for 11%

profile of v1, /device:TPU:0, one launch (start us, length us, event | category | flops | bytes accessed | tf_op | source)
XLA Modules:
  0.0 185.2 jit_solution(15715295726221398688)
XLA Ops:
  7.4 0.0 all-gather.2.cloned.1.call-start
  7.4 0.7 all-gather.2.cloned.1.call-update
  8.1 0.0 all-reduce.2.cloned.1.call-start
  8.8 2.2 %broadcast_select_fusion = bf16[2048,1024]{1,0:T(8,128)(2,1)} fusion(bf16[2048,1024]{1,0:T(8,128)(2,1)} %param.10, pred[]{:T(512)S(6)} %eq.52), kind=kLoop, calls=%fused_computation.5 | loop fusion | flops 2097152 | bytes 8388609 | tf_op jit(solution)/shard_map/jit(_where)/select_n | solution.py:20
  11.0 0.0 copy-start
  11.0 0.0 copy-start.2
  11.0 0.0 all-reduce.2.cloned.1.call-update
  11.1 1.2 copy-done
  12.3 1.1 reshape.50.q_ref
  13.3 0.0 copy-done.2
  13.3 0.2 convert_reduce_fusion
  13.5 0.0 copy-start.1
  13.5 20.4 %shard_map.100 = (f32[4,8,128,128]{3,2,1,0:T(8,128)}, f32[4,8,128,128]{3,2,1,0:T(8,128)}, f32[4,8,128,128]{3,2,1,0:T(8,128)}) custom-call(s32[32]{0:T(128)} %len_ref.1, bf16[128,4096]{1,0:T(8,128)(2,1)} %reshape.50.q_ref, bf16[32,256,1024]{2,1,0:T(8,128)(2,1)} %page_ref.1), custom_call_target="tpu_custom_call" | custom-call | flops 2147483648 | bytes 16777216 | tf_op jit(solution)/shard_map/pallas_call | solution.py:76
  33.9 11.8 %all-gather.2.cloned.1.call-done = bf16[32,4,8192]{2,1,0:T(4,128)(2,1)} async-done(((bf16[32,4,4096]{2,1,0:T(4,128)(2,1)}), bf16[32,4,8192]{2,1,0:T(4,128)(2,1)}) %all-gather.2.cloned.1.call-update) | async-done | bytes 2097168 | tf_op jit(solution)/shard_map/all_gather | solution.py:170
  45.7 2.8 %fusion = f32[32,4]{1,0:T(8,128)S(1)} fusion(bf16[32,4,8192]{2,1,0:T(4,128)(2,1)} %all-gather.2.cloned.1.call-done), kind=kLoop, calls=%fused_computation.2 | loop fusion | flops 3145600 | bytes 2097664 | tf_op jit(solution)/shard_map/reduce_sum | solution.py:173
  48.6 0.0 copy-done.1
  48.6 4.4 %fusion.2 = bf16[32,4,8192]{2,1,0:T(4,128)(2,1)} fusion(bf16[32,4,8192]{2,1,0:T(4,128)(2,1)} %all-gather.2.cloned.1.call-done, f32[8192]{0:T(1024)S(1)} %copy-done.1, f32[32,4]{1,0:T(8,128)S(1)} %add_rsqrt_fusion), kind=kLoop, calls=%fused_computation.4 | loop fusion | flops 4194304 | bytes 4227584 | tf_op jit(solution)/shard_map/convert_element_type | solution.py:175
  53.0 2.5 %reshape.51 = bf16[128,8192]{1,0:T(8,128)(2,1)S(1)} reshape(bf16[32,4,8192]{2,1,0:T(4,128)(2,1)} %fusion.2) | data formatting | bytes 4194304 | tf_op jit(solution)/shard_map/reshape | solution.py:176
  55.5 5.4 %convolution_convert_fusion.1.nk_ref = bf16[128,512]{1,0:T(8,128)(2,1)} fusion(bf16[128,8192]{1,0:T(8,128)(2,1)S(1)} %reshape.51, bf16[8192,512]{1,0:T(8,128)(2,1)} %param.17), kind=kOutput, calls=%fused_computation.7 | convolution fusion | flops 1073807360 | bytes 10616832 | tf_op jit(solution)/shard_map/dot_general | solution.py:177
  61.0 5.3 %convolution_convert_fusion.nv_ref = bf16[128,512]{1,0:T(8,128)(2,1)} fusion(bf16[128,8192]{1,0:T(8,128)(2,1)S(1)} %reshape.51, bf16[8192,512]{1,0:T(8,128)(2,1)} %param.18), kind=kOutput, calls=%fused_computation.6 | convolution fusion | flops 1073807360 | bytes 10616832 | tf_op jit(solution)/shard_map/dot_general | solution.py:178
  66.3 59.9 %all-reduce.2.cloned.1.call-done.kv_ref = bf16[2048,1024]{1,0:T(8,128)(2,1)} async-done(((bf16[2048,1024]{1,0:T(8,128)(2,1)}), bf16[2048,1024]{1,0:T(8,128)(2,1)}) %all-reduce.2.cloned.1.call-update) | async-done | bytes 4194320 | tf_op jit(solution)/shard_map/psum | solution.py:21
  126.2 19.1 %shard_map.101 = bf16[128,4096]{1,0:T(8,128)(2,1)} custom-call(bf16[128,4096]{1,0:T(8,128)(2,1)} %reshape.50.q_ref, bf16[2048,1024]{1,0:T(8,128)(2,1)} %all-reduce.2.cloned.1.call-done.kv_ref, bf16[128,512]{1,0:T(8,128)(2,1)} %convolution_convert_fusion.1.nk_ref, bf16[128,512]{1,0:T(8,128)(2,1)} %convolution_convert_fusion.nv_ref, ...), custom_call_target="tpu_custom_call" | custom-call | flops 4294967296 | bytes 4194304 | tf_op jit(solution)/shard_map/pallas_call | solution.py:134
  145.3 1.9 %reshape.52 = bf16[32,16384]{1,0:T(8,128)(2,1)S(1)} reshape(bf16[128,4096]{1,0:T(8,128)(2,1)} %shard_map.101) | data formatting | bytes 2097152 | tf_op jit(solution)/shard_map/reshape | solution.py:193
  147.2 0.5 fusion.3
  147.7 0.8 copy.23
  148.5 28.3 %all_to_all.5 = bf16[16,2,4,4096]{3,2,1,0:T(4,128)(2,1)S(1)} all-to-all(bf16[16,2,4,4096]{3,2,1,0:T(4,128)(2,1)S(1)} %copy.23), channel_id=1, replica_groups=mesh['dp'=16,'tensor'=2] {'dp'}, dimensions={0} | all-to-all | bytes 2097152 | tf_op jit(solution)/shard_map/all_to_all | solution.py:195
  176.8 1.0 copy.34
  (3 shorter events, 0.0 us)
Async XLA Ops:
  7.4 38.4 %all-gather.2.cloned.1.call-start = ((), (), s32[]{:S(2)}) async-start(), calls=%async_computation.2 | async-start | bytes 3145728 | tf_op jit(solution)/shard_map/all_gather | solution.py:170
  8.1 118.1 %all-reduce.2.cloned.1.call-start = ((), (), s32[]{:S(2)}) async-start(), calls=%async_computation.1 | async-start | bytes 8388608 | tf_op jit(solution)/shard_map/psum | solution.py:21
  11.0 1.2 copy-start
  11.0 2.3 %copy-start.2 = (s32[32,1]{0,1:T(1,128)S(1)}, s32[32,1]{0,1:T(1,128)}, u32[]{:S(2)}) copy-start(s32[32,1]{0,1:T(1,128)} %param.14) | copy-start | bytes 388
  13.5 35.0 %copy-start.1 = (f32[8192]{0:T(1024)S(1)}, f32[8192]{0:T(1024)}, u32[]{:S(2)}) copy-start(f32[8192]{0:T(1024)} %param.16) | copy-start | bytes 98308
Sparse Core Ops, SparseCore 0:
  9.8 35.8 all-gather.1
Sparse Core Ops, SparseCore 1:
  12.2 113.9 all-reduce.1

commit v2 on v0

v2 whole, which is shorter than its diff:
```python
import functools
import math

import jax
import jax.numpy as jnp
from jax import lax
from jax.experimental import pallas as pl
from jax.experimental.pallas import tpu as pltpu
from jax.sharding import PartitionSpec as P

HEAD_SIZE = 128
CAP = 2
epsilon = 1e-05
SCALE2 = math.log2(math.e) / math.sqrt(HEAD_SIZE)
VMEM_LIMIT = 56 * 1024 * 1024
NT = (((1,), (1,)), ((), ()))


def bit(index, b):
    return (index // 2**b) % 2


def kernel(
    steps,
    levels,
    ranks,
    len_ref,
    owner_ref,
    q_ref,
    page_ref,
    x_ref,
    gain_ref,
    wk_ref,
    wv_ref,
    sel_ref,
    prefix_ref,
    out_ref,
    work,
    full,
    x_all,
    acc_ref,
    top_ref,
    sum_ref,
    nk_sum,
    nv_sum,
    square_sum,
    nk_ref,
    nv_ref,
    outgoing,
    copy_sem,
    send_sem,
    recv_sem,
    x_send,
    x_recv,
    o_send,
    o_recv,
    own_sem,
    *landing,
):
    i = pl.program_id(0)
    me = lax.axis_index("dp")
    rank = lax.axis_index("tensor")
    members = 2**levels
    tokens, width = q_ref.shape
    length = prefix_ref.shape[0]
    key_heads = work.shape[0]
    group = width // (key_heads * HEAD_SIZE)
    span = page_ref.shape[1]
    page_steps = tokens // 16
    chunks, _, chunk = gain_ref.shape
    own_chunks = chunks // ranks
    head_width = group * HEAD_SIZE
    final_step = page_steps + chunks + key_heads - 1
    stages = 2 * levels

    def low(b, first):
        start = 0
        for a in range(first, b + 1):
            start = start + bit(me, a) * (length >> (a + 1))
        return start

    def rows(start, size):
        return pl.ds(pl.multiple_of(start, size), size)

    def transfer(k, j):
        if k < levels:
            b = k
            size = length >> (b + 1)
            if b == 0:
                start = (1 - bit(me, 0)) * size
                source = prefix_ref.at[rows(start, size), j * 2 * HEAD_SIZE : (j + 1) * 2 * HEAD_SIZE]
            else:
                start = low(b - 1, 1) + (1 - bit(me, b)) * size
                source = work.at[j, rows(start, size), :]
            target = landing[b].at[j]
        else:
            b = stages - 1 - k
            size = length >> (b + 1)
            source = full.at[j, rows(low(b, 0), size), :]
            target = source
        partner = me + (1 - 2 * bit(me, b)) * 2**b
        return pltpu.make_async_remote_copy(
            src_ref=source,
            dst_ref=target,
            send_sem=send_sem.at[k, j],
            recv_sem=recv_sem.at[k, j],
            device_id={"dp": partner},
            device_id_type=pl.DeviceIdType.MESH,
        )

    def kept(j):
        size = length // 2
        return pltpu.make_async_copy(
            prefix_ref.at[rows(bit(me, 0) * size, size), j * 2 * HEAD_SIZE : (j + 1) * 2 * HEAD_SIZE],
            work.at[j],
            copy_sem.at[j],
        )

    def x_transfer(p, c):
        peer = lax.rem(rank + p, ranks)
        return pltpu.make_async_remote_copy(
            src_ref=x_ref.at[:, c * chunk : (c + 1) * chunk],
            dst_ref=x_all.at[rank * own_chunks + c],
            send_sem=x_send.at[p - 1, c],
            recv_sem=x_recv.at[p - 1, c],
            device_id={"tensor": peer},
            device_id_type=pl.DeviceIdType.MESH,
        )

    def out_transfer(j, p):
        dest = lax.rem(me + p, members)
        return pltpu.make_async_remote_copy(
            src_ref=outgoing.at[j, dest],
            dst_ref=out_ref.at[me, :, j * head_width : (j + 1) * head_width],
            send_sem=o_send.at[j, p],
            recv_sem=o_recv.at[j, p],
            device_id={"dp": dest},
            device_id_type=pl.DeviceIdType.MESH,
        )

    def own_out(j):
        return pltpu.make_async_copy(
            outgoing.at[j, me],
            out_ref.at[me, :, j * head_width : (j + 1) * head_width],
            own_sem.at[j],
        )

    def advance(k, j):
        transfer(k, j).wait_recv()
        if k < levels:
            b = k
            size = length >> (b + 1)
            if b == 0:
                kept(j).wait()
            span_rows = rows(low(b, 1), size)
            mine = work[j, span_rows, :]
            other = landing[b][j]
            side = jnp.zeros(mine.shape, jnp.int32) + owner_ref[0]
            away = ((side // 2**b) % 2 - bit(me, b)).astype(jnp.float32)
            away = (away * away).astype(jnp.bfloat16)
            merged = mine * (1 - away) + other * away
            if b < levels - 1:
                work[j, span_rows, :] = merged
            else:
                full[j, rows(low(b, 0), size), :] = merged
        if k < stages - 1:
            transfer(k + 1, j).start()

    @pl.when(i == 0)
    def _():
        barrier = pltpu.get_barrier_semaphore()

        def greet(p, carry):
            pl.semaphore_signal(
                barrier,
                inc=1,
                device_id={"dp": lax.rem(me + p, members)},
                device_id_type=pl.DeviceIdType.MESH,
            )
            return carry

        lax.fori_loop(1, members, greet, 0)
        for p in range(1, ranks):
            pl.semaphore_signal(
                barrier,
                inc=1,
                device_id={"tensor": lax.rem(rank + p, ranks)},
                device_id_type=pl.DeviceIdType.MESH,
            )
        for j in range(key_heads):
            kept(j).start()
        pl.semaphore_wait(barrier, members - 1 + ranks - 1)
        for j in range(key_heads):
            transfer(0, j).start()
        for p in range(1, ranks):
            for c in range(own_chunks):
                x_transfer(p, c).start()
        for c in range(own_chunks):
            x_all[rank * own_chunks + c] = x_ref[:, c * chunk : (c + 1) * chunk]
        nk_sum[...] = jnp.zeros_like(nk_sum)
        nv_sum[...] = jnp.zeros_like(nv_sum)
        square_sum[...] = jnp.zeros_like(square_sum)

    @pl.when(i < page_steps)
    def _():
        per_pair = 8 // steps
        queries = q_ref[pl.ds(pl.multiple_of(i * 16, 16), 16), :].astype(jnp.float32)
        count = group * 8
        keys = per_pair * span
        row = lax.broadcasted_iota(jnp.int32, (count, keys), 0)
        col = lax.broadcasted_iota(jnp.int32, (count, keys), 1)
        holder = (row % 8) // steps
        for p in range(2):
            limit = jnp.zeros((count, keys), jnp.int32)
            for k in range(per_pair):
                used = len_ref[i * (16 // steps) + p * per_pair + k]
                limit = jnp.where(holder == k, used, limit)
            place = col - holder * span
            visible = (place >= 0) & (place < limit)
            base = p * per_pair
            spot = pl.ds(pl.multiple_of(i * 16 + p * 8, 8), 8)
            for j in range(key_heads):
                q = jnp.concatenate(
                    [
                        queries[
                            p * 8 : p * 8 + 8,
                            (j * group + g) * HEAD_SIZE : (j * group + g + 1) * HEAD_SIZE,
                        ]
                        for g in range(group)
                    ],
                    axis=0,
                ).astype(jnp.bfloat16)
                c = 2 * j * HEAD_SIZE
                k = page_ref[base : base + per_pair, :, c : c + HEAD_SIZE].reshape(keys, HEAD_SIZE)
                v = page_ref[base : base + per_pair, :, c + HEAD_SIZE : c + 2 * HEAD_SIZE]
                v = v.reshape(keys, HEAD_SIZE)
                s = lax.dot_general(q, k, NT, preferred_element_type=jnp.float32)
                s = jnp.where(visible, s, -jnp.inf)
                top = jnp.max(s, axis=1, keepdims=True)
                e = jnp.exp2((s - top) * SCALE2)
                total = jnp.sum(e, axis=1, keepdims=True)
                acc = jnp.dot(e.astype(jnp.bfloat16), v, preferred_element_type=jnp.float32)
                top = jnp.broadcast_to(top, acc.shape)
                total = jnp.broadcast_to(total, acc.shape)
                for g in range(group):
                    acc_ref[j, g, spot, :] = acc[g * 8 : g * 8 + 8]
                    top_ref[j, g, spot, :] = top[g * 8 : g * 8 + 8]
                    sum_ref[j, g, spot, :] = total[g * 8 : g * 8 + 8]

    @pl.when(i == page_steps)
    def _():
        for p in range(1, ranks):
            for c in range(own_chunks):
                x_transfer(p, c).wait()

    @pl.when((i >= page_steps) & (i < page_steps + chunks))
    def _():
        c = i - page_steps
        x = x_all[c].astype(jnp.float32)
        square_sum[...] += jnp.sum(x * x, axis=1, keepdims=True)
        scaled = (x * gain_ref[c]).astype(jnp.bfloat16)
        nk_sum[...] += jnp.dot(scaled, wk_ref[...], preferred_element_type=jnp.float32)
        nv_sum[...] += jnp.dot(scaled, wv_ref[...], preferred_element_type=jnp.float32)

    @pl.when(i == page_steps + chunks - 1)
    def _():
        inverse = lax.rsqrt(square_sum[:, :1] / (chunks * chunk) + epsilon)
        nk = (nk_sum[...] * inverse).astype(jnp.bfloat16)
        nv = (nv_sum[...] * inverse).astype(jnp.bfloat16)
        for j in range(key_heads):
            nk_ref[j] = nk[:, j * HEAD_SIZE : (j + 1) * HEAD_SIZE]
            nv_ref[j] = nv[:, j * HEAD_SIZE : (j + 1) * HEAD_SIZE]

    def attend(j):
        keys = full[j, :, :HEAD_SIZE]
        values = full[j, :, HEAD_SIZE:]
        wide = 2
        row = lax.broadcasted_iota(jnp.int32, (wide * tokens, tokens), 0) % tokens
        col = lax.broadcasted_iota(jnp.int32, (wide * tokens, tokens), 1)
        visible = (row // steps == col // steps) & (col <= row)
        for g in range(0, group, wide):
            first = j * head_width + g * HEAD_SIZE
            q = jnp.concatenate(
                [
                    q_ref[:, first + w * HEAD_SIZE : first + (w + 1) * HEAD_SIZE]
                    for w in range(wide)
                ],
                axis=0,
            )
            paged = jnp.concatenate([acc_ref[j, g + w] for w in range(wide)], axis=0)
            paged_top = jnp.concatenate([top_ref[j, g + w][:, :1] for w in range(wide)], axis=0)
            paged_sum = jnp.concatenate([sum_ref[j, g + w][:, :1] for w in range(wide)], axis=0)
            s = lax.dot_general(q, keys, NT, preferred_element_type=jnp.float32)
            r = lax.dot_general(q, nk_ref[j], NT, preferred_element_type=jnp.float32)
            r = jnp.where(visible, r, -jnp.inf)
            top = jnp.maximum(jnp.max(s, axis=1, keepdims=True), jnp.max(r, axis=1, keepdims=True))
            top = jnp.maximum(top, paged_top)
            e = jnp.exp2((s - top) * SCALE2)
            f = jnp.exp2((r - top) * SCALE2)
            keep = jnp.exp2((paged_top - top) * SCALE2)
            total = (
                jnp.sum(e, axis=1, keepdims=True)
                + jnp.sum(f, axis=1, keepdims=True)
                + keep * paged_sum
            )
            acc = jnp.dot(e.astype(jnp.bfloat16), values, preferred_element_type=jnp.float32)
            acc += jnp.dot(f.astype(jnp.bfloat16), nv_ref[j], preferred_element_type=jnp.float32)
            acc = ((acc + keep * paged) / total).astype(jnp.bfloat16)
            both = jnp.concatenate([acc[w * tokens : (w + 1) * tokens] for w in range(wide)], axis=1)
            placed = jnp.dot(sel_ref[...], both, preferred_element_type=jnp.float32)
            outgoing[j, :, :, g * HEAD_SIZE : (g + wide) * HEAD_SIZE] = placed.reshape(
                members, CAP * steps, wide * HEAD_SIZE
            ).astype(jnp.bfloat16)

    for j in range(key_heads):

        @pl.when(i == page_steps + chunks + j)
        def _(j=j):
            attend(j)

            def send(p, carry):
                out_transfer(j, p).start()
                return carry

            lax.fori_loop(1, members, send, 0)
            own_out(j).start()

    for t in range(stages + key_heads - 1):
        if t < page_steps:
            when = t
        else:
            when = page_steps + (t - page_steps) * 4 + 1

        @pl.when(i == when)
        def _(t=t):
            for j in range(key_heads):
                if 0 <= t - j < stages:
                    advance(t - j, j)

    @pl.when(i == final_step)
    def _():
        for j in range(key_heads):
            for k in range(stages):
                transfer(k, j).wait_send()

            def finish(p, carry):
                out_transfer(j, p).wait()
                return carry

            lax.fori_loop(1, members, finish, 0)
            own_out(j).wait()


def per_device(
    prefix_kv,
    page_key_values,
    context_len,
    prefill_owner,
    assign,
    x_new,
    norm_gain,
    key_weight,
    value_weight,
    decoded_queries,
):
    row_count, steps, width = decoded_queries.shape
    tokens = row_count * steps
    members = lax.axis_size("dp")
    ranks = lax.axis_size("tensor")
    levels = members.bit_length() - 1
    assigned = assign[:, 0]
    indices = jnp.arange(row_count)
    matching = (assigned[:, None] == assigned[None, :]) & (indices[None, :] < indices[:, None])
    ranking = jnp.sum(matching.astype(jnp.int32), axis=1)
    destination = assigned * CAP + ranking
    token_place = (destination[:, None] * steps + jnp.arange(steps)[None, :]).reshape(tokens)
    slots = members * CAP * steps
    selector = (jnp.arange(slots)[:, None] == token_place[None, :]).astype(jnp.bfloat16)

    length, kv_width = prefix_kv.shape
    span = page_key_values.shape[1]
    key_heads = kv_width // (2 * HEAD_SIZE)
    group = width // (key_heads * HEAD_SIZE)
    chunk = min(1024, width)
    chunks = ranks * width // chunk
    page_steps = tokens // 16
    new_width = key_weight.shape[1]

    def whole(*shape):
        return pl.BlockSpec(shape, lambda i: (0,) * len(shape))

    weight = pl.BlockSpec((chunk, new_width), lambda i: (jnp.clip(i - page_steps, 0, chunks - 1), 0))
    stat = pltpu.VMEM((key_heads, group, tokens, HEAD_SIZE), jnp.float32)
    decoded = pl.pallas_call(
        functools.partial(kernel, steps, levels, ranks),
        grid=(page_steps + chunks + key_heads,),
        in_specs=[
            pl.BlockSpec(memory_space=pltpu.SMEM),
            pl.BlockSpec(memory_space=pltpu.SMEM),
            whole(tokens, width),
            pl.BlockSpec(
                (16 // steps, span, kv_width), lambda i: (jnp.minimum(i, page_steps - 1), 0, 0)
            ),
            whole(tokens, width),
            whole(chunks, 1, chunk),
            weight,
            weight,
            whole(slots, tokens),
            pl.BlockSpec(memory_space=pl.ANY),
        ],
        out_specs=pl.BlockSpec(memory_space=pl.ANY),
        out_shape=jax.ShapeDtypeStruct((members, CAP * steps, width), jnp.bfloat16),
        scratch_shapes=[
            pltpu.VMEM((key_heads, length // 2, 2 * HEAD_SIZE), jnp.bfloat16),
            pltpu.VMEM((key_heads, length, 2 * HEAD_SIZE), jnp.bfloat16),
            pltpu.VMEM((chunks, tokens, chunk), jnp.bfloat16),
            stat,
            stat,
            stat,
            pltpu.VMEM((tokens, new_width), jnp.float32),
            pltpu.VMEM((tokens, new_width), jnp.float32),
            pltpu.VMEM((tokens, HEAD_SIZE), jnp.float32),
            pltpu.VMEM((key_heads, tokens, HEAD_SIZE), jnp.bfloat16),
            pltpu.VMEM((key_heads, tokens, HEAD_SIZE), jnp.bfloat16),
            pltpu.VMEM((key_heads, members, CAP * steps, group * HEAD_SIZE), jnp.bfloat16),
            pltpu.SemaphoreType.DMA((key_heads,)),
            pltpu.SemaphoreType.DMA((2 * levels, key_heads)),
            pltpu.SemaphoreType.DMA((2 * levels, key_heads)),
            pltpu.SemaphoreType.DMA((ranks - 1, width // chunk)),
            pltpu.SemaphoreType.DMA((ranks - 1, width // chunk)),
            pltpu.SemaphoreType.DMA((key_heads, members)),
            pltpu.SemaphoreType.DMA((key_heads, members)),
            pltpu.SemaphoreType.DMA((key_heads,)),
        ]
        + [
            pltpu.VMEM((key_heads, length >> (b + 1), 2 * HEAD_SIZE), jnp.bfloat16)
            for b in range(levels)
        ],
        compiler_params=pltpu.CompilerParams(
            collective_id=0,
            has_side_effects=True,
            vmem_limit_bytes=VMEM_LIMIT,
            dimension_semantics=("arbitrary",),
        ),
        cost_estimate=pl.CostEstimate(
            flops=4 * tokens * length * width, bytes_accessed=2 * page_key_values.size, transcendentals=0
        ),
    )(
        context_len,
        prefill_owner,
        decoded_queries.reshape(tokens, width),
        page_key_values,
        x_new.reshape(tokens, width),
        norm_gain.reshape(chunks, 1, chunk),
        key_weight,
        value_weight,
        selector,
        prefix_kv,
    )
    return decoded.reshape(members * CAP, steps, width)


def solution(mesh):
    in_specs = (
        P("dp", "tensor"),
        P("dp", None, "tensor"),
        P("dp"),
        P(),
        P("dp", None),
        P("dp", None, "tensor"),
        P(),
        P(None, "tensor"),
        P(None, "tensor"),
        P("dp", None, "tensor"),
    )
    out_specs = P("dp", None, "tensor")
    return jax.shard_map(
        per_device, mesh=mesh, in_specs=in_specs, out_specs=out_specs, check_vma=False
    )
```

time: 678 us -> 110 us (0.16); the launches traced: 669 us -> 110 us
  waiting for transfers between devices: 448 us -> 0 us
  Pallas kernels: 0 us -> 99.9 us
  matrix products: 83.9 us -> 0 us
  local copies, waits for them, and re-layouts: 66.2 us -> 6.63 us
  starting transfers between devices: 26.5 us -> 0 us
  other arithmetic: 28.7 us -> 2.27 us
  between operations: 16.2 us -> 0.67 us
    psum x1 -> x0, waiting for transfers between devices: 419 us -> none  [broadcast(): return lax.psum(block, axis)]
    pallas_call x0 -> x1, Pallas kernels: none -> 99.9 us  [per_device(): pl.pallas_call(functools.partial(kernel, steps, levels, ranks), grid=(pag...]
    dot_general x12 -> x0, matrix products: 83.9 us -> none  [the longest x4 27.1 us: to_slots(): jnp.dot(selector, payload.reshape(row_count, -1), preferred_element_type=...]
    all_to_all x4 -> x0, starting transfers between devices: 26.2 us -> none  [the longest x1 7.39 us: per_device(): lax.all_to_all(to_slots(request_lengths), 'dp', split_axis=0, concat_axis...]
    all_gather x1 -> x0, waiting for transfers between devices: 22.3 us -> none  [per_device(): lax.all_gather(x_new, 'tensor', axis=2, tiled=True).astype(jnp.float32)]
    dot_general x5 -> x0, local copies, waits for them, and re-layouts: 22.2 us -> none  [to_slots(): jnp.dot(selector, payload.reshape(row_count, -1), preferred_element_type=...]
    all_to_all x1 -> x0, local copies, waits for them, and re-layouts: 21.5 us -> none  [per_device(): lax.all_to_all(to_slots(page_key_values), 'dp', split_axis=0, concat_axis...]
    reduce_sum x4 -> x0, other arithmetic: 21.3 us -> none  [the longest x1 14.3 us: attend(): jnp.sum(shared_exp, axis=-1, keepdims=True)]
  transfers between devices with their start and end apart: 6 -> 0, of which waited for: 3 -> 0; matrix products, arithmetic and copies ran while one was open for 16% -> 0% of each run, Pallas kernels for 0% -> 0%
where the time goes in v2:
time: 110 us
  Pallas kernels  99.9 us (91%)
  local copies, waits for them, and re-layouts  6.63 us (6%)
  other arithmetic  2.27 us (2%)
    pallas_call x1, Pallas kernels, per_device(): pl.pallas_call(functools.partial(kernel, steps, levels, ranks), grid=(pag...  99.9 us
    reshape x1, local copies, waits for them, and re-layouts, per_device(): return decoded.reshape(members * CAP, steps, width)  2.24 us

profile of v2, /device:TPU:0, one launch (start us, length us, event | category | flops | bytes accessed | tf_op | source)
XLA Modules:
  0.0 109.5 jit_solution(17277649302749085137)
XLA Ops:
  0.7 0.9 convert_reduce_fusion
  1.6 0.7 fusion.3
  2.2 0.1 iota_add_fusion
  2.3 0.1 add.31
  2.4 0.6 fusion.sel_ref
  3.0 2.2 %reshape.30.x_ref = bf16[128,4096]{1,0:T(8,128)(2,1)} reshape(bf16[32,4,4096]{2,1,0:T(4,128)(2,1)} %param.15) | data formatting | bytes 2097152 | tf_op jit(solution)/shard_map/reshape | solution.py:453
  5.2 2.1 %reshape.29.q_ref = bf16[128,4096]{1,0:T(8,128)(2,1)} reshape(bf16[32,4,4096]{2,1,0:T(4,128)(2,1)} %param.19) | data formatting | bytes 2097152 | tf_op jit(solution)/shard_map/reshape | solution.py:451
  7.3 99.9 %shard_map.100 = bf16[16,8,4096]{2,1,0:T(8,128)(2,1)} custom-call(s32[32]{0:T(128)} %len_ref.1, s32[1]{0:T(128)S(6)} %copy.11.owner_ref, bf16[128,4096]{1,0:T(8,128)(2,1)} %reshape.29.q_ref, bf16[32,256,1024]{2,1,0:T(8,128)(2,1)} %page_ref.1, bf16[128,4096]{1,0:T(8,128)(2,1)} %reshape.30.x_ref, f32[8,1,1024]{2,1,0:T(1,128)} %bitcast.10, ...), custom_call_target="tpu_custom_call" | custom-call | flops 4294967296 | bytes 16777216 | tf_op jit(solution)/shard_map/pallas_call | solution.py:394
  107.3 2.2 %reshape.32 = bf16[32,4,4096]{2,1,0:T(4,128)(2,1)} reshape(bf16[16,8,4096]{2,1,0:T(8,128)(2,1)} %shard_map.100) | data formatting | bytes 2097152 | tf_op jit(solution)/shard_map/reshape | solution.py:460

commit v3 on v2

--- a/solution.py
+++ b/solution.py
@@ -26,7 +26,7 @@
     ranks,
     len_ref,
     owner_ref,
-    q_ref,
+    q_in,
     page_ref,
     x_ref,
     gain_ref,
@@ -35,6 +35,7 @@
     sel_ref,
     prefix_ref,
     out_ref,
+    q_ref,
     work,
     full,
     x_all,
@@ -43,7 +44,7 @@
     sum_ref,
     nk_sum,
     nv_sum,
-    square_sum,
+    inverse_ref,
     nk_ref,
     nv_ref,
     outgoing,
@@ -73,6 +74,9 @@
     final_step = page_steps + chunks + key_heads - 1
     stages = 2 * levels
 
+    def flat(block):
+        return block.astype(jnp.float32).reshape(tokens, block.shape[-1])
+
     def low(b, first):
         start = 0
         for a in range(first, b + 1):
@@ -119,7 +123,7 @@
     def x_transfer(p, c):
         peer = lax.rem(rank + p, ranks)
         return pltpu.make_async_remote_copy(
-            src_ref=x_ref.at[:, c * chunk : (c + 1) * chunk],
+            src_ref=x_ref.at[:, :, c * chunk : (c + 1) * chunk],
             dst_ref=x_all.at[rank * own_chunks + c],
             send_sem=x_send.at[p - 1, c],
             recv_sem=x_recv.at[p - 1, c],
@@ -131,7 +135,7 @@
         dest = lax.rem(me + p, members)
         return pltpu.make_async_remote_copy(
             src_ref=outgoing.at[j, dest],
-            dst_ref=out_ref.at[me, :, j * head_width : (j + 1) * head_width],
+            dst_ref=out_ref.at[pl.ds(me * CAP, CAP), :, j * head_width : (j + 1) * head_width],
             send_sem=o_send.at[j, p],
             recv_sem=o_recv.at[j, p],
             device_id={"dp": dest},
@@ -141,7 +145,7 @@
     def own_out(j):
         return pltpu.make_async_copy(
             outgoing.at[j, me],
-            out_ref.at[me, :, j * head_width : (j + 1) * head_width],
+            out_ref.at[pl.ds(me * CAP, CAP), :, j * head_width : (j + 1) * head_width],
             own_sem.at[j],
         )
 
@@ -196,10 +200,13 @@
             for c in range(own_chunks):
                 x_transfer(p, c).start()
         for c in range(own_chunks):
-            x_all[rank * own_chunks + c] = x_ref[:, c * chunk : (c + 1) * chunk]
+            x_all[rank * own_chunks + c] = x_ref[:, :, c * chunk : (c + 1) * chunk]
+        for c in range(own_chunks):
+            q_ref[:, c * chunk : (c + 1) * chunk] = flat(
+                q_in[:, :, c * chunk : (c + 1) * chunk]
+            ).astype(jnp.bfloat16)
         nk_sum[...] = jnp.zeros_like(nk_sum)
         nv_sum[...] = jnp.zeros_like(nv_sum)
-        square_sum[...] = jnp.zeros_like(square_sum)
 
     @pl.when(i < page_steps)
     def _():
@@ -252,21 +259,24 @@
         for p in range(1, ranks):
             for c in range(own_chunks):
                 x_transfer(p, c).wait()
+        squares = jnp.zeros((tokens, 1), jnp.float32)
+        for c in range(chunks):
+            x = flat(x_all[c])
+            squares += jnp.sum(x * x, axis=1, keepdims=True)
+        inverse = lax.rsqrt(squares / (chunks * chunk) + epsilon)
+        inverse_ref[...] = jnp.broadcast_to(inverse, inverse_ref.shape)
 
     @pl.when((i >= page_steps) & (i < page_steps + chunks))
     def _():
         c = i - page_steps
-        x = x_all[c].astype(jnp.float32)
-        square_sum[...] += jnp.sum(x * x, axis=1, keepdims=True)
-        scaled = (x * gain_ref[c]).astype(jnp.bfloat16)
+        scaled = (flat(x_all[c]) * inverse_ref[:, :1] * gain_ref[c]).astype(jnp.bfloat16)
         nk_sum[...] += jnp.dot(scaled, wk_ref[...], preferred_element_type=jnp.float32)
         nv_sum[...] += jnp.dot(scaled, wv_ref[...], preferred_element_type=jnp.float32)
 
     @pl.when(i == page_steps + chunks - 1)
     def _():
-        inverse = lax.rsqrt(square_sum[:, :1] / (chunks * chunk) + epsilon)
-        nk = (nk_sum[...] * inverse).astype(jnp.bfloat16)
-        nv = (nv_sum[...] * inverse).astype(jnp.bfloat16)
+        nk = nk_sum[...].astype(jnp.bfloat16)
+        nv = nv_sum[...].astype(jnp.bfloat16)
         for j in range(key_heads):
             nk_ref[j] = nk[:, j * HEAD_SIZE : (j + 1) * HEAD_SIZE]
             nv_ref[j] = nv[:, j * HEAD_SIZE : (j + 1) * HEAD_SIZE]
@@ -308,8 +318,8 @@
             acc = ((acc + keep * paged) / total).astype(jnp.bfloat16)
             both = jnp.concatenate([acc[w * tokens : (w + 1) * tokens] for w in range(wide)], axis=1)
             placed = jnp.dot(sel_ref[...], both, preferred_element_type=jnp.float32)
-            outgoing[j, :, :, g * HEAD_SIZE : (g + wide) * HEAD_SIZE] = placed.reshape(
-                members, CAP * steps, wide * HEAD_SIZE
+            outgoing[j, :, :, :, g * HEAD_SIZE : (g + wide) * HEAD_SIZE] = placed.reshape(
+                members, CAP, steps, wide * HEAD_SIZE
             ).astype(jnp.bfloat16)
 
     for j in range(key_heads):
@@ -326,10 +336,10 @@
             own_out(j).start()
 
     for t in range(stages + key_heads - 1):
-        if t < page_steps:
-            when = t
+        if t < stages:
+            when = t * (page_steps + chunks - 1) // (stages - 1)
         else:
-            when = page_steps + (t - page_steps) * 4 + 1
+            when = page_steps + chunks + t - stages
 
         @pl.when(i == when)
         def _(t=t):
@@ -397,11 +407,11 @@
         in_specs=[
             pl.BlockSpec(memory_space=pltpu.SMEM),
             pl.BlockSpec(memory_space=pltpu.SMEM),
-            whole(tokens, width),
+            whole(row_count, steps, width),
             pl.BlockSpec(
                 (16 // steps, span, kv_width), lambda i: (jnp.minimum(i, page_steps - 1), 0, 0)
             ),
-            whole(tokens, width),
+            whole(row_count, steps, width),
             whole(chunks, 1, chunk),
             weight,
             weight,
@@ -409,11 +419,12 @@
             pl.BlockSpec(memory_space=pl.ANY),
         ],
         out_specs=pl.BlockSpec(memory_space=pl.ANY),
-        out_shape=jax.ShapeDtypeStruct((members, CAP * steps, width), jnp.bfloat16),
+        out_shape=jax.ShapeDtypeStruct((members * CAP, steps, width), jnp.bfloat16),
         scratch_shapes=[
+            pltpu.VMEM((tokens, width), jnp.bfloat16),
             pltpu.VMEM((key_heads, length // 2, 2 * HEAD_SIZE), jnp.bfloat16),
             pltpu.VMEM((key_heads, length, 2 * HEAD_SIZE), jnp.bfloat16),
-            pltpu.VMEM((chunks, tokens, chunk), jnp.bfloat16),
+            pltpu.VMEM((chunks, row_count, steps, chunk), jnp.bfloat16),
             stat,
             stat,
             stat,
@@ -422,7 +433,7 @@
             pltpu.VMEM((tokens, HEAD_SIZE), jnp.float32),
             pltpu.VMEM((key_heads, tokens, HEAD_SIZE), jnp.bfloat16),
             pltpu.VMEM((key_heads, tokens, HEAD_SIZE), jnp.bfloat16),
-            pltpu.VMEM((key_heads, members, CAP * steps, group * HEAD_SIZE), jnp.bfloat16),
+            pltpu.VMEM((key_heads, members, CAP, steps, group * HEAD_SIZE), jnp.bfloat16),
             pltpu.SemaphoreType.DMA((key_heads,)),
             pltpu.SemaphoreType.DMA((2 * levels, key_heads)),
             pltpu.SemaphoreType.DMA((2 * levels, key_heads)),
@@ -448,16 +459,16 @@
     )(
         context_len,
         prefill_owner,
-        decoded_queries.reshape(tokens, width),
+        decoded_queries,
         page_key_values,
-        x_new.reshape(tokens, width),
+        x_new,
         norm_gain.reshape(chunks, 1, chunk),
         key_weight,
         value_weight,
         selector,
         prefix_kv,
     )
-    return decoded.reshape(members * CAP, steps, width)
+    return decoded
 
 
 def solution(mesh):

time: 110 us -> 98.7 us (0.90)
  Pallas kernels: 99.9 us -> 91.9 us
  local copies, waits for them, and re-layouts: 6.63 us -> 2.93 us
    pallas_call x1, Pallas kernels: 99.9 us -> 91.9 us  [per_device(): pl.pallas_call(functools.partial(kernel, steps, levels, ranks), grid=(pag...]
    reshape x3 -> x0, local copies, waits for them, and re-layouts: 6.52 us -> none  [the longest x1 2.24 us: per_device(): return decoded.reshape(members * CAP, steps, width)]
    unnamed x0 -> x1, local copies, waits for them, and re-layouts: none -> 2.82 us
where the time goes in v3:
time: 98.7 us; the launch traced here: 97.8 us
  Pallas kernels  91.9 us (93%)
  local copies, waits for them, and re-layouts  2.93 us (3%)
  other arithmetic  2.28 us (2%)
    pallas_call x1, Pallas kernels, per_device(): pl.pallas_call(functools.partial(kernel, steps, levels, ranks), grid=(pag...  91.9 us
    unnamed x1, local copies, waits for them, and re-layouts  2.82 us

profile of v3, /device:TPU:0, one launch (start us, length us, event | category | flops | bytes accessed | tf_op | source)
XLA Modules:
  0.0 97.8 jit_solution(7930240532933461474)
XLA Ops:
  0.7 0.9 convert_reduce_fusion
  1.6 0.7 fusion.3
  2.2 0.1 iota_add_fusion
  2.3 0.1 add.31
  2.4 0.6 fusion.sel_ref
  3.0 91.9 %shard_map.100 = bf16[32,4,4096]{2,1,0:T(4,128)(2,1)} custom-call(s32[32]{0:T(128)} %len_ref.1, s32[1]{0:T(128)S(6)} %copy.12.owner_ref, bf16[32,4,4096]{2,1,0:T(4,128)(2,1)} %q_in.1, bf16[32,256,1024]{2,1,0:T(8,128)(2,1)} %page_ref.1, bf16[32,4,4096]{2,1,0:T(4,128)(2,1)} %x_ref.1, f32[8,1,1024]{2,1,0:T(1,128)} %bitcast.10, bf16[8192,512]{1,0:T(8,128)(2,1)} %wk_ref.1, ...), custom_call_target="tpu_custom_call" | custom-call | flops 4294967296 | bytes 16777216 | tf_op jit(solution)/shard_map/pallas_call | solution.py:404
  94.9 2.8 %copy.13 = bf16[32,4,4096]{2,1,0:T(4,128)(2,1)} copy(bf16[32,4,4096]{2,1,0:T(4,128)(2,1)} %shard_map.100) | data formatting | bytes 2097152

commit v4 on v3

--- a/solution.py
+++ b/solution.py
@@ -343,8 +343,11 @@
 
         @pl.when(i == when)
         def _(t=t):
-            for j in range(key_heads):
-                if 0 <= t - j < stages:
+            late = t - (stages - 2)
+            if t >= stages:
+                advance(stages - 2, late - 1)
+            for j in reversed(range(key_heads)):
+                if 0 <= t - j < stages and not (t >= stages - 1 and j == late):
                     advance(t - j, j)
 
     @pl.when(i == final_step)

time: 98.7 us -> 99.3 us (level)
  Pallas kernels: 91.9 us -> 93.2 us
    pallas_call x1, Pallas kernels: 91.9 us -> 93.2 us  [per_device(): pl.pallas_call(functools.partial(kernel, steps, levels, ranks), grid=(pag...]
where the time goes in v4:
time: 99.3 us; the launch traced here: 99.1 us
  Pallas kernels  93.2 us (94%)
  local copies, waits for them, and re-layouts  2.93 us (3%)
  other arithmetic  2.28 us (2%)
    pallas_call x1, Pallas kernels, per_device(): pl.pallas_call(functools.partial(kernel, steps, levels, ranks), grid=(pag...  93.2 us
    unnamed x1, local copies, waits for them, and re-layouts  2.82 us

profile of v4, /device:TPU:0, one launch (start us, length us, event | category | flops | bytes accessed | tf_op | source)
XLA Modules:
  0.0 99.1 jit_solution(5369370141146965997)
XLA Ops:
  0.7 0.9 convert_reduce_fusion
  1.6 0.7 fusion.3
  2.2 0.1 iota_add_fusion
  2.3 0.1 add.31
  2.4 0.6 fusion.sel_ref
  3.0 93.2 %shard_map.100 = bf16[32,4,4096]{2,1,0:T(4,128)(2,1)} custom-call(s32[32]{0:T(128)} %len_ref.1, s32[1]{0:T(128)S(6)} %copy.12.owner_ref, bf16[32,4,4096]{2,1,0:T(4,128)(2,1)} %q_in.1, bf16[32,256,1024]{2,1,0:T(8,128)(2,1)} %page_ref.1, bf16[32,4,4096]{2,1,0:T(4,128)(2,1)} %x_ref.1, f32[8,1,1024]{2,1,0:T(1,128)} %bitcast.10, bf16[8192,512]{1,0:T(8,128)(2,1)} %wk_ref.1, ...), custom_call_target="tpu_custom_call" | custom-call | flops 4294967296 | bytes 16777216 | tf_op jit(solution)/shard_map/pallas_call | solution.py:407
  96.3 2.8 %copy.13 = bf16[32,4,4096]{2,1,0:T(4,128)(2,1)} copy(bf16[32,4,4096]{2,1,0:T(4,128)(2,1)} %shard_map.100) | data formatting | bytes 2097152
